TPU v7x, 32 devices: a whole 2x2x4 slice. The times are simulated.
32 devices in a mesh: grp: 4 (over z), dev: 8 (over y, x, core).
Axes of the slice: x: 2, y: 2, z: 4, core: 2. Of those that a mesh axis runs over, the one named last changes fastest.
Arguments:
- old_fields: float32 [3, 256, 32, 1024], P(None, ('grp', 'dev')), as said below
- old_counts: int32 [32], replicated, may hold values from 2 to 6, as said below
Outputs:
- pressure_out: float32 [128, 256, 128], P('grp', 'dev')
- residual: float32 [128, 256, 128], P('grp', 'dev')
Inputs may be any that keep to these rules, and one draw needn't show every extreme that they name: `old_counts`: the counts sum to 128; each device's first box number, start[e], lies between e * 4 and e * 4 + 4 / 2; the slots of a device beyond its count hold data that belongs to no box. `old_fields`: coefficient entries (component 2) are positive; components 0 and 1 are real-valued of order one.
All inputs are finite; a program needn't handle non-finite values.
Results may differ from a plain program's by a relative error of at most 0.0003.
Values sent between devices are 32-bit elements; how exact they have to be, the bound alone decides.
A program may use at most 64 MiB of HBM per device.

v0:
```python
import jax
import jax.numpy as jnp
from jax import lax
from jax.sharding import PartitionSpec as P


def from_behind(value, axis, steps):
    count = lax.axis_size(axis)
    leading, last = (max(0, -steps), min(count, count - steps))
    return lax.ppermute(value, axis, [(source, source + steps) for source in range(leading, last)])


def extended(array, sides, width):
    for axis, dim in sides:
        size, length = (lax.axis_size(axis), array.shape[dim])
        up = [(i, (i + 1) % size) for i in range(size - 1)]
        down = [(j, i) for i, j in up]
        last = lax.slice_in_dim(array, length - width, length, axis=dim)
        leading = lax.slice_in_dim(array, 0, width, axis=dim)
        before = lax.ppermute(last, axis, up)
        after = lax.ppermute(leading, axis, down)
        array = jnp.concatenate([before, array, after], axis=dim)
    return array


def shifted_slices(padded):
    sizes = (padded.shape[0] - 2, padded.shape[1] - 2, padded.shape[2] - 2)
    pieces = []
    for axis_id in range(3):
        for offset in (0, 2):
            starts = [1, 1, 1]
            starts[axis_id] = offset
            pieces.append(lax.dynamic_slice(padded, starts, sizes))
    return pieces


def beta_phi(padded_phi, betas):
    total = jnp.zeros(betas[0].shape, jnp.float32)
    for beta, neighbour in zip(betas, shifted_slices(padded_phi)):
        total = total + beta * neighbour
    return total


def per_device(old_fields, old_counts):
    slot_count = old_fields.shape[1]
    box_edge = old_fields.shape[2]
    box_count = slot_count // 2
    device_id = lax.axis_index("grp") * lax.axis_size("dev") + lax.axis_index("dev")
    ends = jnp.cumsum(old_counts)
    starts = jnp.concatenate([jnp.zeros((1,), jnp.int32), ends])
    wanted = device_id * box_count + jnp.arange(box_count, dtype=jnp.int32)
    own_start = starts[device_id]
    is_below = wanted < own_start
    owner_dev = device_id - is_below.astype(jnp.int32)
    local_slot = wanted - starts[owner_dev]
    prev_start = starts[jnp.maximum(device_id - 1, 0)]
    half_count = box_count // 2
    send_start = jnp.clip((device_id + 1) * box_count - own_start, 0, slot_count - half_count)
    tail_part = lax.dynamic_slice_in_dim(old_fields, send_start, half_count, 1)
    from_lower = from_behind(tail_part, ("grp", "dev"), 1)
    recv_start = jnp.clip(device_id * box_count - prev_start, 0, slot_count - half_count)
    lower_slot = local_slot - recv_start
    lower_rows = jnp.take(from_lower, jnp.clip(lower_slot, 0, from_lower.shape[1] - 1), axis=1)
    own_rows = jnp.take(old_fields, jnp.clip(local_slot, 0, slot_count - 1), axis=1)
    moved = jnp.where(is_below[None, :, None, None], lower_rows, own_rows)
    moved = moved.reshape(3, box_count, box_edge, box_edge, box_edge)
    moved = jnp.transpose(moved, (0, 2, 3, 1, 4)).reshape(
        3, box_edge, box_edge, box_count * box_edge
    )
    pressure = moved[0]
    right_side = moved[1]
    coefficient = moved[2]
    padded = extended(jnp.stack([pressure, coefficient]), (("grp", 1), ("dev", 2)), 1)
    padded = jnp.pad(padded, ((0, 0), (0, 0), (0, 0), (1, 1)))
    betas = [0.5 * (coefficient + neighbour) for neighbour in shifted_slices(padded[1])]
    beta_sum = betas[0]
    for beta in betas[1:]:
        beta_sum = beta_sum + beta
    shape = pressure.shape
    parity = (
        lax.broadcasted_iota(jnp.int32, shape, 0)
        + lax.broadcasted_iota(jnp.int32, shape, 1)
        + lax.broadcasted_iota(jnp.int32, shape, 2)
    ) % 2
    red_mask = parity == 0
    first = jnp.where(red_mask, (right_side + beta_phi(padded[0], betas)) / beta_sum, pressure)
    padded_first = extended(first, (("grp", 0), ("dev", 1)), 1)
    padded_first = jnp.pad(padded_first, ((0, 0), (0, 0), (1, 1)))
    second = jnp.where(red_mask, first, (right_side + beta_phi(padded_first, betas)) / beta_sum)
    padded_second = extended(second, (("grp", 0), ("dev", 1)), 1)
    padded_second = jnp.pad(padded_second, ((0, 0), (0, 0), (1, 1)))
    residual = right_side - (beta_sum * second - beta_phi(padded_second, betas))
    return (second, residual)


def solution(mesh):
    placed = (P(None, ("grp", "dev"), None, None), P())
    return jax.shard_map(
        per_device,
        mesh=mesh,
        in_specs=placed,
        out_specs=(P("grp", "dev", None), P("grp", "dev", None)),
        check_vma=False,
    )
```

profile of v0, /device:TPU:3, one launch (start us, length us, event | category | flops | bytes accessed | tf_op | source)
XLA Modules:
  0.0 123.9 jit_solution(12493452408356059897)
XLA Ops:
  4.1 3.7 %collective-permute-start = (f32[3,2,32,1024]{3,2,1,0:T(8,128)}, f32[3,2,32,1024]{3,2,1,0:T(8,128)}, u32[]{:S(2)}, u32[]{:S(2)}) collective-permute-start(f32[3,2,32,1024]{3,2,1,0:T(8,128)} %constant_dynamic-slice_fusion), channel_id=1, source_target_pairs={{0,1},{1,2},{2,3},{3,4},{4,5},{5,6},{6,7},{7,8},{8,9},{9,10},{10,1... | collective-permute-start | bytes 2359304 | tf_op jit(solution)/shard_map/ppermute | solution.py:10
  11.5 5.3 %gather.22 = f32[3,4,32,32,32]{4,3,2,0,1:T(8,128)} reshape(f32[3,4,32,1024]{3,2,0,1:T(8,128)} %bitcast.32) | data formatting | bytes 3145728 | tf_op jit(solution)/shard_map/jit(_take)/gather | solution.py:64
  17.5 2.9 %gather_fusion.1 = f32[4,3,32,1024]{3,2,1,0:T(8,128)} fusion(f32[3,2,32,1024]{3,2,1,0:T(8,128)} %collective-permute-done, s32[1024]{0:T(1024)S(1)} %pad_clamp_fusion.1), kind=kCustom, calls=%fused_computation.1 | custom fusion | bytes 3145744 | tf_op jit(solution)/shard_map/jit(_take)/gather | solution.py:63
  20.5 5.3 %gather.20 = f32[3,4,32,32,32]{4,3,2,0,1:T(8,128)} reshape(f32[3,4,32,1024]{3,2,0,1:T(8,128)} %bitcast.31) | data formatting | bytes 3145728 | tf_op jit(solution)/shard_map/jit(_take)/gather | solution.py:63
  25.8 15.4 %fusion.1 = f32[3,32,32,4,32]{4,3,2,1,0:T(4,128)S(1)} fusion(f32[3,4,32,32,32]{4,3,2,0,1:T(8,128)} %gather.22, f32[3,4,32,32,32]{4,3,2,0,1:T(8,128)} %gather.20, pred[4]{0:T(512)(128)(4,1)S(1)} %get-tuple-element.20, pred[4]{0:T(512)(128)(4,1)S(1)} %get-tuple-element.19, pred[4]{0:T(512)(128)(4,1)S(1)} %fusion.48), kind=kLoop, calls=%fused_computation.5 | loop fusion | flops 1179648 | bytes 4718604 | tf_op jit(solution)/shard_map/transpose | solution.py:67
  41.2 2.8 %fusion.49 = (f32[1,32,32,4,32]{4,3,2,1,0:T(4,128)}, f32[1,32,32,4,32]{4,3,2,1,0:T(4,128)}, f32[1,32,32,4,32]{4,3,2,1,0:T(4,128)}) fusion(f32[3,32,32,4,32]{4,3,2,1,0:T(4,128)S(1)} %fusion.1), kind=kLoop, calls=%fused_computation.135 | loop fusion | bytes 3145728 | tf_op jit(solution)/shard_map/slice | solution.py:72
  44.0 3.1 %slice.82 = f32[1,32,32,128]{3,2,1,0:T(8,128)} reshape(f32[1,32,32,4,32]{4,3,2,1,0:T(4,128)} %get-tuple-element.2) | data formatting | bytes 1048576 | tf_op jit(solution)/shard_map/slice | solution.py:72
  47.1 3.1 %slice.81 = f32[1,32,32,128]{3,2,1,0:T(8,128)} reshape(f32[1,32,32,4,32]{4,3,2,1,0:T(4,128)} %get-tuple-element.3) | data formatting | bytes 1048576 | tf_op jit(solution)/shard_map/slice | solution.py:70
  52.3 3.2 %collective-permute-start.1 = (f32[2,1,32,128]{3,2,1,0:T(8,128)S(1)}, f32[2,1,32,128]{3,2,1,0:T(8,128)S(1)}, u32[]{:S(2)}, u32[]{:S(2)}) collective-permute-start(f32[2,1,32,128]{3,2,1,0:T(8,128)S(1)} %get-tuple-element.9), channel_id=1, source_target_pairs={{0,8},{8,16},{16,24},{1,9},{9,17},{17,25},{2,10},{10,18},{18,26},{... | collective-permute-start | bytes 98312 | tf_op jit(solution)/shard_map/ppermute | solution.py:20
  56.8 3.3 %collective-permute-done.2 = f32[2,1,32,128]{3,2,1,0:T(8,128)S(1)} collective-permute-done((f32[2,1,32,128]{3,2,1,0:T(8,128)S(1)}, f32[2,1,32,128]{3,2,1,0:T(8,128)S(1)}, u32[]{:S(2)}, u32[]{:S(2)}) %collective-permute-start.2) | collective-permute-done | bytes 32800 | tf_op jit(solution)/shard_map/ppermute | solution.py:21
  60.2 6.2 %collective-permute-start.3 = (f32[2,34,1,128]{3,2,1,0:T(1,128)S(1)}, f32[2,34,1,128]{3,2,1,0:T(1,128)S(1)}, u32[]{:S(2)}, u32[]{:S(2)}) collective-permute-start(f32[2,34,1,128]{3,2,1,0:T(1,128)S(1)} %get-tuple-element.7), channel_id=1, source_target_pairs={{0,1},{1,2},{2,3},{3,4},{4,5},{5,6},{6,7},{8,9},{9,10},{10,11},{11... | collective-permute-start | bytes 104456 | tf_op jit(solution)/shard_map/ppermute | solution.py:20
  66.4 2.1 %collective-permute-start.4 = (f32[2,34,1,128]{3,2,1,0:T(1,128)S(1)}, f32[2,34,1,128]{3,2,1,0:T(1,128)S(1)}, u32[]{:S(2)}, u32[]{:S(2)}) collective-permute-start(f32[2,34,1,128]{3,2,1,0:T(1,128)S(1)} %get-tuple-element.8), channel_id=1, source_target_pairs={{1,0},{2,1},{3,2},{4,3},{5,4},{6,5},{7,6},{9,8},{10,9},{11,10},{12... | collective-permute-start | bytes 104456 | tf_op jit(solution)/shard_map/ppermute | solution.py:21
  68.5 3.1 %squeeze.24 = f32[32,32,128]{2,1,0:T(8,128)} reshape(f32[1,32,32,4,32]{4,3,2,1,0:T(4,128)} %get-tuple-element.2) | data formatting | bytes 1048576 | tf_op jit(solution)/shard_map/squeeze | solution.py:72
  71.6 3.1 %squeeze.27 = f32[32,32,128]{2,1,0:T(8,128)} reshape(f32[1,32,32,4,32]{4,3,2,1,0:T(4,128)} %get-tuple-element.3) | data formatting | bytes 1048576 | tf_op jit(solution)/shard_map/squeeze | solution.py:70
  74.7 3.1 %squeeze.23 = f32[32,32,128]{2,1,0:T(8,128)} reshape(f32[1,32,32,4,32]{4,3,2,1,0:T(4,128)} %get-tuple-element.4) | data formatting | bytes 1048576 | tf_op jit(solution)/shard_map/squeeze | solution.py:71
  77.7 2.3 %select_maximum_fusion = f32[2,34,34,130]{3,2,1,0:T(8,128)S(1)} fusion(f32[2,34,1,128]{3,2,1,0:T(1,128)S(1)} %collective-permute-done.4, f32[2,34,1,128]{3,2,1,0:T(1,128)S(1)} %collective-permute-done.3, f32[2,1,32,128]{3,2,1,0:T(8,128)S(1)} %collective-permute-done.2, f32[2,32,32,128]{3,2,1,0:T(8,128)} %copy-done.4, ...), kind=kLoop, calls=%fused_computation.9 | loop fusion | flops 3606720 | bytes 2385984 | tf_op jit(solution)/shard_map/concatenate | solution.py:22
  82.9 3.2 %collective-permute-start.5 = (f32[1,32,128]{2,1,0:T(8,128)S(1)}, f32[1,32,128]{2,1,0:T(8,128)S(1)}, u32[]{:S(2)}, u32[]{:S(2)}) collective-permute-start(f32[1,32,128]{2,1,0:T(8,128)S(1)} %get-tuple-element.17), channel_id=1, source_target_pairs={{0,8},{8,16},{16,24},{1,9},{9,17},{17,25},{2,10},{10,18},{18,26},{... | collective-permute-start | bytes 49160 | tf_op jit(solution)/shard_map/ppermute | solution.py:20
  87.4 3.2 %collective-permute-done.6 = f32[1,32,128]{2,1,0:T(8,128)S(1)} collective-permute-done((f32[1,32,128]{2,1,0:T(8,128)S(1)}, f32[1,32,128]{2,1,0:T(8,128)S(1)}, u32[]{:S(2)}, u32[]{:S(2)}) %collective-permute-start.6) | collective-permute-done | bytes 16416 | tf_op jit(solution)/shard_map/ppermute | solution.py:21
  90.6 6.0 %collective-permute-start.7 = (f32[34,1,128]{2,1,0:T(1,128)S(1)}, f32[34,1,128]{2,1,0:T(1,128)S(1)}, u32[]{:S(2)}, u32[]{:S(2)}) collective-permute-start(f32[34,1,128]{2,1,0:T(1,128)S(1)} %get-tuple-element.13), channel_id=1, source_target_pairs={{0,1},{1,2},{2,3},{3,4},{4,5},{5,6},{6,7},{8,9},{9,10},{10,11},{11... | collective-permute-start | bytes 52232 | tf_op jit(solution)/shard_map/ppermute | solution.py:20
  98.5 4.0 %collective-permute-done.8 = f32[34,1,128]{2,1,0:T(1,128)S(1)} collective-permute-done((f32[34,1,128]{2,1,0:T(1,128)S(1)}, f32[34,1,128]{2,1,0:T(1,128)S(1)}, u32[]{:S(2)}, u32[]{:S(2)}) %collective-permute-start.8) | collective-permute-done | bytes 17440 | tf_op jit(solution)/shard_map/ppermute | solution.py:21
  104.4 3.2 %collective-permute-start.9 = (f32[1,32,128]{2,1,0:T(8,128)S(1)}, f32[1,32,128]{2,1,0:T(8,128)S(1)}, u32[]{:S(2)}, u32[]{:S(2)}) collective-permute-start(f32[1,32,128]{2,1,0:T(8,128)S(1)} %get-tuple-element.15), channel_id=1, source_target_pairs={{0,8},{8,16},{16,24},{1,9},{9,17},{17,25},{2,10},{10,18},{18,26},{... | collective-permute-start | bytes 49160 | tf_op jit(solution)/shard_map/ppermute | solution.py:20
  108.9 3.2 %collective-permute-done.10 = f32[1,32,128]{2,1,0:T(8,128)S(1)} collective-permute-done((f32[1,32,128]{2,1,0:T(8,128)S(1)}, f32[1,32,128]{2,1,0:T(8,128)S(1)}, u32[]{:S(2)}, u32[]{:S(2)}) %collective-permute-start.10) | collective-permute-done | bytes 16416 | tf_op jit(solution)/shard_map/ppermute | solution.py:21
  112.1 3.4 %collective-permute-start.11 = (f32[34,1,128]{2,1,0:T(1,128)S(1)}, f32[34,1,128]{2,1,0:T(1,128)S(1)}, u32[]{:S(2)}, u32[]{:S(2)}) collective-permute-start(f32[34,1,128]{2,1,0:T(1,128)S(1)} %get-tuple-element.11), channel_id=1, source_target_pairs={{0,1},{1,2},{2,3},{3,4},{4,5},{5,6},{6,7},{8,9},{9,10},{10,11},{11... | collective-permute-start | bytes 52232 | tf_op jit(solution)/shard_map/ppermute | solution.py:20
  117.4 4.0 %collective-permute-done.12 = f32[34,1,128]{2,1,0:T(1,128)S(1)} collective-permute-done((f32[34,1,128]{2,1,0:T(1,128)S(1)}, f32[34,1,128]{2,1,0:T(1,128)S(1)}, u32[]{:S(2)}, u32[]{:S(2)}) %collective-permute-start.12) | collective-permute-done | bytes 17440 | tf_op jit(solution)/shard_map/ppermute | solution.py:21
  (54 shorter events, 23.5 us)
Async XLA Ops:
  0.6 2.4 %copy-start = (f32[3,8,32,1024]{3,2,1,0:T(8,128)S(1)}, f32[3,8,32,1024]{3,2,1,0:T(8,128)}, u32[]{:S(2)}) copy-start(f32[3,8,32,1024]{3,2,1,0:T(8,128)} %param.2) | copy-start | bytes 9437188
  4.1 13.4 %collective-permute-start = (f32[3,2,32,1024]{3,2,1,0:T(8,128)}, f32[3,2,32,1024]{3,2,1,0:T(8,128)}, u32[]{:S(2)}, u32[]{:S(2)}) collective-permute-start(f32[3,2,32,1024]{3,2,1,0:T(8,128)} %constant_dynamic-slice_fusion), channel_id=1, source_target_pairs={{0,1},{1,2},{2,3},{3,4},{4,5},{5,6},{6,7},{7,8},{8,9},{9,10},{10,1... | collective-permute-start | bytes 2359304 | tf_op jit(solution)/shard_map/ppermute | solution.py:10
  52.3 7.9 %copy-start.4 = (f32[2,32,32,128]{3,2,1,0:T(8,128)}, f32[2,32,32,128]{3,2,1,0:T(8,128)S(1)}, u32[]{:S(2)}) copy-start(f32[2,32,32,128]{3,2,1,0:T(8,128)S(1)} %constant_dynamic-update-slice_fusion) | copy-start | bytes 3145732
  52.3 4.5 %collective-permute-start.1 = (f32[2,1,32,128]{3,2,1,0:T(8,128)S(1)}, f32[2,1,32,128]{3,2,1,0:T(8,128)S(1)}, u32[]{:S(2)}, u32[]{:S(2)}) collective-permute-start(f32[2,1,32,128]{3,2,1,0:T(8,128)S(1)} %get-tuple-element.9), channel_id=1, source_target_pairs={{0,8},{8,16},{16,24},{1,9},{9,17},{17,25},{2,10},{10,18},{18,26},{... | collective-permute-start | bytes 98312 | tf_op jit(solution)/shard_map/ppermute | solution.py:20
  55.5 4.7 %collective-permute-start.2 = (f32[2,1,32,128]{3,2,1,0:T(8,128)S(1)}, f32[2,1,32,128]{3,2,1,0:T(8,128)S(1)}, u32[]{:S(2)}, u32[]{:S(2)}) collective-permute-start(f32[2,1,32,128]{3,2,1,0:T(8,128)S(1)} %get-tuple-element.10), channel_id=1, source_target_pairs={{8,0},{16,8},{24,16},{9,1},{17,9},{25,17},{10,2},{18,10},{26,18},{... | collective-permute-start | bytes 98312 | tf_op jit(solution)/shard_map/ppermute | solution.py:21
  60.2 17.5 %collective-permute-start.3 = (f32[2,34,1,128]{3,2,1,0:T(1,128)S(1)}, f32[2,34,1,128]{3,2,1,0:T(1,128)S(1)}, u32[]{:S(2)}, u32[]{:S(2)}) collective-permute-start(f32[2,34,1,128]{3,2,1,0:T(1,128)S(1)} %get-tuple-element.7), channel_id=1, source_target_pairs={{0,1},{1,2},{2,3},{3,4},{4,5},{5,6},{6,7},{8,9},{9,10},{10,11},{11... | collective-permute-start | bytes 104456 | tf_op jit(solution)/shard_map/ppermute | solution.py:20
  66.4 11.3 %collective-permute-start.4 = (f32[2,34,1,128]{3,2,1,0:T(1,128)S(1)}, f32[2,34,1,128]{3,2,1,0:T(1,128)S(1)}, u32[]{:S(2)}, u32[]{:S(2)}) collective-permute-start(f32[2,34,1,128]{3,2,1,0:T(1,128)S(1)} %get-tuple-element.8), channel_id=1, source_target_pairs={{1,0},{2,1},{3,2},{4,3},{5,4},{6,5},{7,6},{9,8},{10,9},{11,10},{12... | collective-permute-start | bytes 104456 | tf_op jit(solution)/shard_map/ppermute | solution.py:21
  80.1 1.0 copy-start.2
  80.1 1.2 copy-start.3
  80.1 1.3 %copy-start.5 = (f32[32,32,128]{2,1,0:T(8,128)S(1)}, f32[32,32,128]{2,1,0:T(8,128)}, u32[]{:S(2)}) copy-start(f32[32,32,128]{2,1,0:T(8,128)} %squeeze.27) | copy-start | bytes 1572868
  82.9 4.5 %collective-permute-start.5 = (f32[1,32,128]{2,1,0:T(8,128)S(1)}, f32[1,32,128]{2,1,0:T(8,128)S(1)}, u32[]{:S(2)}, u32[]{:S(2)}) collective-permute-start(f32[1,32,128]{2,1,0:T(8,128)S(1)} %get-tuple-element.17), channel_id=1, source_target_pairs={{0,8},{8,16},{16,24},{1,9},{9,17},{17,25},{2,10},{10,18},{18,26},{... | collective-permute-start | bytes 49160 | tf_op jit(solution)/shard_map/ppermute | solution.py:20
  86.1 4.5 %collective-permute-start.6 = (f32[1,32,128]{2,1,0:T(8,128)S(1)}, f32[1,32,128]{2,1,0:T(8,128)S(1)}, u32[]{:S(2)}, u32[]{:S(2)}) collective-permute-start(f32[1,32,128]{2,1,0:T(8,128)S(1)} %get-tuple-element.18), channel_id=1, source_target_pairs={{8,0},{16,8},{24,16},{9,1},{17,9},{25,17},{10,2},{18,10},{26,18},{... | collective-permute-start | bytes 49160 | tf_op jit(solution)/shard_map/ppermute | solution.py:21
  90.6 7.9 %collective-permute-start.7 = (f32[34,1,128]{2,1,0:T(1,128)S(1)}, f32[34,1,128]{2,1,0:T(1,128)S(1)}, u32[]{:S(2)}, u32[]{:S(2)}) collective-permute-start(f32[34,1,128]{2,1,0:T(1,128)S(1)} %get-tuple-element.13), channel_id=1, source_target_pairs={{0,1},{1,2},{2,3},{3,4},{4,5},{5,6},{6,7},{8,9},{9,10},{10,11},{11... | collective-permute-start | bytes 52232 | tf_op jit(solution)/shard_map/ppermute | solution.py:20
  96.6 6.0 %collective-permute-start.8 = (f32[34,1,128]{2,1,0:T(1,128)S(1)}, f32[34,1,128]{2,1,0:T(1,128)S(1)}, u32[]{:S(2)}, u32[]{:S(2)}) collective-permute-start(f32[34,1,128]{2,1,0:T(1,128)S(1)} %get-tuple-element.14), channel_id=1, source_target_pairs={{1,0},{2,1},{3,2},{4,3},{5,4},{6,5},{7,6},{9,8},{10,9},{11,10},{12... | collective-permute-start | bytes 52232 | tf_op jit(solution)/shard_map/ppermute | solution.py:21
  104.3 19.6 %copy-start.1 = (f32[32,32,128]{2,1,0:T(8,128)}, f32[32,32,128]{2,1,0:T(8,128)S(1)}, u32[]{:S(2)}) copy-start(f32[32,32,128]{2,1,0:T(8,128)S(1)} %fusion.20) | copy-start | bytes 1572868
  104.4 4.5 %collective-permute-start.9 = (f32[1,32,128]{2,1,0:T(8,128)S(1)}, f32[1,32,128]{2,1,0:T(8,128)S(1)}, u32[]{:S(2)}, u32[]{:S(2)}) collective-permute-start(f32[1,32,128]{2,1,0:T(8,128)S(1)} %get-tuple-element.15), channel_id=1, source_target_pairs={{0,8},{8,16},{16,24},{1,9},{9,17},{17,25},{2,10},{10,18},{18,26},{... | collective-permute-start | bytes 49160 | tf_op jit(solution)/shard_map/ppermute | solution.py:20
  107.6 4.5 %collective-permute-start.10 = (f32[1,32,128]{2,1,0:T(8,128)S(1)}, f32[1,32,128]{2,1,0:T(8,128)S(1)}, u32[]{:S(2)}, u32[]{:S(2)}) collective-permute-start(f32[1,32,128]{2,1,0:T(8,128)S(1)} %get-tuple-element.16), channel_id=1, source_target_pairs={{8,0},{16,8},{24,16},{9,1},{17,9},{25,17},{10,2},{18,10},{26,18},{... | collective-permute-start | bytes 49160 | tf_op jit(solution)/shard_map/ppermute | solution.py:21
  112.1 5.3 %collective-permute-start.11 = (f32[34,1,128]{2,1,0:T(1,128)S(1)}, f32[34,1,128]{2,1,0:T(1,128)S(1)}, u32[]{:S(2)}, u32[]{:S(2)}) collective-permute-start(f32[34,1,128]{2,1,0:T(1,128)S(1)} %get-tuple-element.11), channel_id=1, source_target_pairs={{0,1},{1,2},{2,3},{3,4},{4,5},{5,6},{6,7},{8,9},{9,10},{10,11},{11... | collective-permute-start | bytes 52232 | tf_op jit(solution)/shard_map/ppermute | solution.py:20
  115.5 6.0 %collective-permute-start.12 = (f32[34,1,128]{2,1,0:T(1,128)S(1)}, f32[34,1,128]{2,1,0:T(1,128)S(1)}, u32[]{:S(2)}, u32[]{:S(2)}) collective-permute-start(f32[34,1,128]{2,1,0:T(1,128)S(1)} %get-tuple-element.12), channel_id=1, source_target_pairs={{1,0},{2,1},{3,2},{4,3},{5,4},{6,5},{7,6},{9,8},{10,9},{11,10},{12... | collective-permute-start | bytes 52232 | tf_op jit(solution)/shard_map/ppermute | solution.py:21
where the time goes:
time: 125 us; the launch traced here: 124 us
  local copies, waits for them, and re-layouts  40.1 us (32%)
  starting transfers between devices  38.6 us (31%)
  other arithmetic  25.1 us (20%)
  waiting for transfers between devices  17.8 us (14%)
  between operations  2.3 us (2%)
    ppermute x6, starting transfers between devices, extended(): before = lax.ppermute(last, axis, up)  25.1 us
    ppermute x6, waiting for transfers between devices, extended(): after = lax.ppermute(leading, axis, down)  17.8 us
    transpose x1, other arithmetic, per_device(): jnp.transpose(moved, (0, 2, 3, 1, 4))  15.4 us
    ppermute x6, starting transfers between devices, extended(): after = lax.ppermute(leading, axis, down)  9.82 us
    gather x2, local copies, waits for them, and re-layouts, per_device(): jnp.take(from_lower, jnp.clip(lower_slot, 0, from_lower.shape[1] - 1), ax...  8.27 us
    gather x2, local copies, waits for them, and re-layouts, per_device(): jnp.take(old_fields, jnp.clip(local_slot, 0, slot_count - 1), axis=1)  7.07 us
    slice x2, local copies, waits for them, and re-layouts, per_device(): coefficient = moved[2]  5.88 us
    ppermute x1, starting transfers between devices, from_behind(): lax.ppermute(value, axis, [(source, source + steps) for source in range(l...  3.67 us
  transfers between devices with their start and end apart: 13, of which 5 were waited for; matrix products, arithmetic and copies ran while one was open for 15% of the time, Pallas kernels for 0%

commit v1 on v0

v1 whole, which is shorter than its diff:
```python
import functools

import jax
import jax.numpy as jnp
from jax import lax
from jax.experimental import pallas as pl
from jax.experimental.pallas import tpu as pltpu
from jax.sharding import PartitionSpec as P

MESH = pl.DeviceIdType.MESH
LANES = 128
TOP = 8


def kernel(n_grp, n_dev, counts, fields, out_p, out_r,
           own_b, own_p, own_f, snd_b, snd_p, snd_f, got_b, got_p, got_f,
           pa, pb, pc, h, f, s, rinv, sx, gx, sh0, sh1, gh0, gh1,
           in_sem, snd_sem, got_sem, hs_sem, hg_sem):
    edge = h.shape[1] - 2 * TOP
    sh, gh = (sh0, sh1), (gh0, gh1)
    grp, dev = lax.axis_index("grp"), lax.axis_index("dev")
    me = grp * n_dev + dev
    last = n_grp * n_dev - 1
    mine = (own_b, own_p, own_f)
    comps = (2, 0, 1)
    loads = []
    for i in range(3):
        copy = pltpu.make_async_copy(
            fields.at[comps[i], pl.ds(0, own_b.shape[0])], mine[i], in_sem.at[i])
        copy.start()
        loads.append(copy)

    has = (dev > 0, dev < n_dev - 1, grp > 0, grp < n_grp - 1)
    peer = ((grp, dev - 1), (grp, dev + 1), (grp - 1, dev), (grp + 1, dev))
    has_prev, has_next = me > 0, me < last
    prev_far = jnp.logical_and(has_prev, dev == 0)
    next_far = jnp.logical_and(has_next, dev == n_dev - 1)
    before, after = me - 1, me + 1
    prev_id = (before // n_dev, before % n_dev)
    next_id = (after // n_dev, after % n_dev)

    barrier = pltpu.get_barrier_semaphore()
    total = jnp.int32(0)
    for flag, target in list(zip(has, peer)) + [(prev_far, prev_id), (next_far, next_id)]:
        total = total + flag.astype(jnp.int32)

        @pl.when(flag)
        def _(target=target):
            pl.semaphore_signal(barrier, inc=1, device_id=target, device_id_type=MESH)

    start = lax.fori_loop(0, me, lambda i, acc: acc + counts[i], jnp.int32(0))
    k = jnp.clip(start - me * 4, 0, 2)

    zero_plane = jnp.zeros(h.shape[1:], jnp.float32)

    def clear(y, _):
        for ref in (pa, pb, pc, h):
            ref[y] = zero_plane
        return 0

    lax.fori_loop(0, edge + 2, clear, 0)
    pl.semaphore_wait(barrier, total)

    lane = lax.broadcasted_iota(jnp.int32, (8, 1024), 1)
    row = lax.broadcasted_iota(jnp.int32, (8, 1024), 0)
    black_box = (row + lane + lane // 32) % 2 == 1

    regrid = [
        pltpu.make_async_remote_copy(
            src_ref=src, dst_ref=dst, send_sem=snd_sem.at[i], recv_sem=got_sem.at[i],
            device_id=next_id, device_id_type=MESH)
        for i, (src, dst) in enumerate(((snd_b, got_b), (snd_p, got_p), (snd_f, got_f)))
    ]
    for i in range(3):
        loads[i].wait()
        for t in range(edge // 8):
            tile = slice(8 * t, 8 * t + 8)
            first, second = mine[i][4 - k, tile, :], mine[i][5 - k, tile, :]
            if i == 1:
                snd_p[tile, :] = jnp.where(black_box, first, pltpu.roll(second, 1, 0))
            else:
                dst = (snd_b, None, snd_f)[i]
                dst[0, tile, :] = first
                dst[1, tile, :] = second

        @pl.when(has_next)
        def _(i=i):
            regrid[i].start()

    block = lax.broadcasted_iota(jnp.int32, (edge, LANES), 1) // 32
    in0, in1, in2 = block == 0, block == 1, block == 2

    def pick(parts):
        return jnp.where(in0, parts[0], jnp.where(in1, parts[1], jnp.where(in2, parts[2], parts[3])))

    def boxes_to_rows(i, yh):
        cols = pl.ds(pl.multiple_of(yh * LANES, LANES), LANES)
        ref = mine[i]
        own = [ref[jnp.maximum(c - k, 0), :, cols] for c in range(4)]
        if i == 1:
            low0 = got_p[:, cols]
            low1 = pltpu.roll(low0.reshape(edge // 8, 8, LANES), 7, 1).reshape(edge, LANES)
        else:
            got = (got_b, None, got_f)[i]
            low0, low1 = got[0, :, cols], got[1, :, cols]
        boxes = [jnp.where(k >= 1, low0, own[0]), jnp.where(k >= 2, low1, own[1]), own[2], own[3]]
        turned = [boxes[0]] + [pltpu.roll(boxes[c], 32 * c, 1) for c in range(1, 4)]
        rows = []
        for j in range(4):
            value = pick([turned[(q - j) % 4] for q in range(4)])
            rows.append(value if j == 0 else pltpu.roll(value, LANES - 32 * j, 1))
        return rows

    for i in range(3):

        @pl.when(has_prev)
        def _(i=i):
            regrid[i].wait_recv()

        def place(yh, _, i=i):
            rows = boxes_to_rows(i, yh)
            for j in range(4):
                y = yh * 4 + j
                if i == 2:
                    f[y] = rows[j]
                else:
                    ref, value, at = (h, 0.5 * rows[j], edge) if i == 0 else (pa, rows[j], 0)
                    ref[y + 1, TOP:TOP + edge, :] = value
                    for side in range(2):
                        sx[side + 2, pl.ds(at + y, 1), :] = (
                            value[0:1] if side == 0 else value[edge - 1:edge])
            return 0

        lax.fori_loop(0, edge // 4, place, 0)
        if i == 1:
            for side in range(2):
                y = 1 if side == 0 else edge
                sx[side, 0:edge, :] = pa[y, TOP:TOP + edge, :]
                sx[side, edge:2 * edge, :] = h[y, TOP:TOP + edge, :]

            def halo(src, dst, slot):
                return [
                    pltpu.make_async_remote_copy(
                        src_ref=src(w), dst_ref=dst(w ^ 1),
                        send_sem=hs_sem.at[slot, w], recv_sem=hg_sem.at[slot, w ^ 1],
                        device_id=peer[w], device_id_type=MESH)
                    for w in range(4)
                ]

            def arrivals(src, dst, slot):
                return [
                    pltpu.make_async_remote_copy(
                        src_ref=src(w), dst_ref=dst(w),
                        send_sem=hs_sem.at[slot, w], recv_sem=hg_sem.at[slot, w],
                        device_id=peer[w], device_id_type=MESH)
                    for w in range(4)
                ]

            def send(src, dst, slot):
                for w, copy in enumerate(halo(src, dst, slot)):
                    pl.when(has[w])(copy.start)

            def receive(src, dst, slot):
                for w, copy in enumerate(arrivals(src, dst, slot)):
                    pl.when(has[w])(copy.wait_recv)

            def finish(src, dst, slot):
                for w, copy in enumerate(halo(src, dst, slot)):
                    pl.when(has[w])(copy.wait_send)

            wide = (lambda w: sx.at[w], lambda w: gx.at[w])
            send(*wide, 0)

    def unpack(src, targets):
        for side in range(2):
            y = 0 if side == 0 else edge + 1

            @pl.when(has[side])
            def _(side=side, y=y):
                for ref, at in targets:
                    ref[y, TOP:TOP + edge, :] = src(side)[at:at + edge, :]

        for side in range(2):
            x = TOP - 1 if side == 0 else TOP + edge

            @pl.when(has[side + 2])
            def _(side=side, x=x):
                def one(y, _):
                    for ref, at in targets:
                        ref[y + 1, x:x + 1, :] = src(side + 2)[pl.ds(at + y, 1), :]
                    return 0

                lax.fori_loop(0, edge, one, 0, unroll=8)

    lanes = lax.broadcasted_iota(jnp.int32, (edge, LANES), 1)
    xs = lax.broadcasted_iota(jnp.int32, (edge, LANES), 0)
    even = (lanes + xs) % 2 == 0
    low_edge, high_edge = lanes == 0, lanes == LANES - 1

    def near(ref, y):
        centre = ref[y + 1, TOP:TOP + edge, :]
        return centre, [
            ref[y + 1, TOP - 1:TOP - 1 + edge, :],
            ref[y + 1, TOP + 1:TOP + 1 + edge, :],
            ref[y, TOP:TOP + edge, :],
            ref[y + 2, TOP:TOP + edge, :],
            jnp.where(low_edge, 0.0, pltpu.roll(centre, 1, 1)),
            jnp.where(high_edge, 0.0, pltpu.roll(centre, LANES - 1, 1)),
        ]

    def sums(ref, y, with_s):
        p0, p_near = near(ref, y)
        h0, h_near = near(h, y)
        flow, weight = None, None
        for p_n, h_n in zip(p_near, h_near):
            beta = h0 + h_n
            flow = beta * p_n if flow is None else flow + beta * p_n
            if with_s:
                weight = beta if weight is None else weight + beta
        return p0, flow, weight

    def pass_over(body):
        def step(i, _):
            for j in range(2):
                body(i * 2 + j, even if j == 0 else jnp.logical_not(even))
            return 0

        lax.fori_loop(0, edge // 2, step, 0)

    def keep(ref, slot, y, value):
        ref[y + 1, TOP:TOP + edge, :] = value
        sh[slot][2, pl.ds(y, 1), :] = value[0:1]
        sh[slot][3, pl.ds(y, 1), :] = value[edge - 1:edge]

    receive(*wide, 0)
    unpack(lambda w: gx.at[w], ((pa, 0), (h, edge)))

    def red(y, mask):
        p0, flow, weight = sums(pa, y, True)
        inverse = 1.0 / weight
        s[y] = weight
        rinv[y] = inverse
        keep(pb, 0, y, jnp.where(mask, (f[y] + flow) * inverse, p0))

    def black(y, mask):
        p0, flow, _ = sums(pb, y, False)
        value = jnp.where(mask, p0, (f[y] + flow) * rinv[y])
        keep(pc, 1, y, value)
        out_p[pl.ds(y, edge, stride=edge), :] = value

    def rest(y, mask):
        p0, flow, _ = sums(pc, y, False)
        out_r[pl.ds(y, edge, stride=edge), :] = f[y] - (s[y] * p0 - flow)

    def exchange(ref, slot):
        for side in range(2):
            y = 1 if side == 0 else edge
            sh[slot][side] = ref[y, TOP:TOP + edge, :]
        ends = (lambda w: sh[slot].at[w], lambda w: gh[slot].at[w])
        send(*ends, slot + 1)
        receive(*ends, slot + 1)
        unpack(lambda w: gh[slot].at[w], ((ref, 0),))

    pass_over(red)
    exchange(pb, 0)
    pass_over(black)
    exchange(pc, 1)
    pass_over(rest)

    for i in range(3):
        @pl.when(has_next)
        def _(i=i):
            regrid[i].wait_send()
    finish(*wide, 0)
    for slot in range(2):
        finish(lambda w: sh[slot].at[w], lambda w: gh[slot].at[w], slot + 1)


def per_device(n_grp, n_dev, old_fields, old_counts):
    slots, edge, width = old_fields.shape[1:]
    held = slots * 3 // 4
    vmem = lambda *shape: pltpu.VMEM(shape, jnp.float32)
    padded = vmem(edge + 2, edge + 2 * TOP, LANES)
    block = vmem(edge, edge, LANES)
    out = jax.ShapeDtypeStruct((edge * edge, LANES), jnp.float32)
    pressure, residual = pl.pallas_call(
        functools.partial(kernel, n_grp, n_dev),
        out_shape=(out, out),
        in_specs=[pl.BlockSpec(memory_space=pltpu.SMEM), pl.BlockSpec(memory_space=pl.ANY)],
        out_specs=[pl.BlockSpec(memory_space=pltpu.VMEM)] * 2,
        scratch_shapes=[vmem(held, edge, width)] * 3
        + [vmem(2, edge, width), vmem(edge, width), vmem(2, edge, width)] * 2
        + [padded] * 4 + [block] * 3
        + [vmem(4, 2 * edge, LANES)] * 2 + [vmem(4, edge, LANES)] * 4
        + [pltpu.SemaphoreType.DMA((3,))] * 3 + [pltpu.SemaphoreType.DMA((3, 4))] * 2,
        compiler_params=pltpu.CompilerParams(
            collective_id=0, has_side_effects=True, vmem_limit_bytes=40 * 1024 * 1024),
        cost_estimate=pl.CostEstimate(
            flops=edge * edge * LANES * 80, bytes_accessed=4 * 1024 * 1024, transcendentals=0),
    )(old_counts, old_fields)
    shape = (edge, edge, LANES)
    return pressure.reshape(shape), residual.reshape(shape)


def solution(mesh):
    placed = (P(None, ("grp", "dev"), None, None), P())
    return jax.shard_map(
        functools.partial(per_device, mesh.shape["grp"], mesh.shape["dev"]),
        mesh=mesh,
        in_specs=placed,
        out_specs=(P("grp", "dev", None), P("grp", "dev", None)),
        check_vma=False,
    )
```

time: 125 us -> 33.8 us (0.27)
  the two profiles are of different devices: /device:TPU:3 before, /device:TPU:0 now
where the time goes in v1:
time: 33.8 us; the launch traced here: 33.7 us
  Pallas kernels  28.9 us (86%)
  local copies, waits for them, and re-layouts  4.13 us (12%)
  between operations  0.65 us (2%)
    pallas_call x1, Pallas kernels, per_device(): pl.pallas_call(functools.partial(kernel, n_grp, n_dev), out_shape=(out, o...  28.9 us
    unnamed x6, local copies, waits for them, and re-layouts  4.13 us

profile of v1, /device:TPU:0, one launch (start us, length us, event | category | flops | bytes accessed | tf_op | source)
XLA Modules:
  0.0 33.7 jit_solution(14480844719076940245)
XLA Ops:
  0.6 0.0 copy-start
  0.6 1.9 %copy-done = f32[3,8,32,1024]{3,2,1,0:T(8,128)S(1)} copy-done((f32[3,8,32,1024]{3,2,1,0:T(8,128)S(1)}, f32[3,8,32,1024]{3,2,1,0:T(8,128)}, u32[]{:S(2)}) %copy-start) | copy-done | bytes 3145752
  2.5 0.0 copy-start.1
  2.5 0.7 %copy-done.1 = s32[32]{0:T(128)S(1)} copy-done((s32[32]{0:T(128)S(1)}, s32[32]{0:T(128)}, u32[]{:S(2)}) %copy-start.1) | copy-done | bytes 152
  3.2 28.9 %shard_map.41 = (f32[1024,128]{1,0:T(8,128)S(1)}, f32[1024,128]{1,0:T(8,128)S(1)}) custom-call(s32[32]{0:T(128)S(1)} %copy-done.1, f32[3,8,32,1024]{3,2,1,0:T(8,128)S(1)} %copy-done), custom_call_target="tpu_custom_call" | custom-call | flops 10485760 | bytes 4194304 | tf_op jit(solution)/shard_map/pallas_call | solution.py:286
  32.1 0.8 %copy.6 = f32[32,32,128]{2,1,0:T(8,128)} copy(f32[32,32,128]{2,1,0:T(8,128)S(1)} %bitcast.3) | data formatting | bytes 1048576
  32.9 0.8 %copy.7 = f32[32,32,128]{2,1,0:T(8,128)} copy(f32[32,32,128]{2,1,0:T(8,128)S(1)} %bitcast.2) | data formatting | bytes 1048576
Async XLA Ops:
  0.6 1.9 %copy-start = (f32[3,8,32,1024]{3,2,1,0:T(8,128)S(1)}, f32[3,8,32,1024]{3,2,1,0:T(8,128)}, u32[]{:S(2)}) copy-start(f32[3,8,32,1024]{3,2,1,0:T(8,128)} %fields.1) | copy-start | bytes 9437188
  2.5 0.7 %copy-start.1 = (s32[32]{0:T(128)S(1)}, s32[32]{0:T(128)}, u32[]{:S(2)}) copy-start(s32[32]{0:T(128)} %counts.1) | copy-start | bytes 388

commit v2 on v1

--- a/solution.py
+++ b/solution.py
@@ -10,11 +10,71 @@
 MESH = pl.DeviceIdType.MESH
 LANES = 128
 TOP = 8
-
-
-def kernel(n_grp, n_dev, counts, fields, out_p, out_r,
+UNROLL = 16
+
+
+def even_cells(edge):
+    lanes = lax.broadcasted_iota(jnp.int32, (edge, LANES), 1)
+    xs = lax.broadcasted_iota(jnp.int32, (edge, LANES), 0)
+    return (lanes + xs) % 2 == 0
+
+
+def near(ref, y):
+    edge = ref.shape[0] - 2
+    lanes = lax.broadcasted_iota(jnp.int32, (edge, LANES), 1)
+    centre = ref[y + 1, TOP:TOP + edge, :]
+    return centre, [
+        ref[y + 1, TOP - 1:TOP - 1 + edge, :],
+        ref[y + 1, TOP + 1:TOP + 1 + edge, :],
+        ref[y, TOP:TOP + edge, :],
+        ref[y + 2, TOP:TOP + edge, :],
+        jnp.where(lanes == 0, 0.0, pltpu.roll(centre, 1, 1)),
+        jnp.where(lanes == LANES - 1, 0.0, pltpu.roll(centre, LANES - 1, 1)),
+    ]
+
+
+def sums(ref, h, y, with_s):
+    p0, p_near = near(ref, y)
+    h0, h_near = near(h, y)
+    flow, weight = None, None
+    for p_n, h_n in zip(p_near, h_near):
+        beta = h0 + h_n
+        flow = beta * p_n if flow is None else flow + beta * p_n
+        if with_s:
+            weight = beta if weight is None else weight + beta
+    return p0, flow, weight
+
+
+def pass_over(edge, body):
+    even = even_cells(edge)
+
+    def step(i, _):
+        for j in range(UNROLL):
+            body(i * UNROLL + j, even if j % 2 == 0 else jnp.logical_not(even))
+        return 0
+
+    lax.fori_loop(0, edge // UNROLL, step, 0)
+
+
+def finish_kernel(pressure, pc, h, f, s, out_p, out_r, stage, sem):
+    edge = f.shape[0]
+    first = pltpu.make_async_copy(pressure, out_p, sem.at[0])
+    first.start()
+
+    def rest(y, mask):
+        p0, flow, _ = sums(pc, h, y, False)
+        stage[pl.ds(y, edge, stride=edge), :] = f[y] - (s[y] * p0 - flow)
+
+    pass_over(edge, rest)
+    second = pltpu.make_async_copy(stage, out_r, sem.at[1])
+    second.start()
+    first.wait()
+    second.wait()
+
+
+def kernel(n_grp, n_dev, counts, fields, out_p, pc, h, f, s,
            own_b, own_p, own_f, snd_b, snd_p, snd_f, got_b, got_p, got_f,
-           pa, pb, pc, h, f, s, rinv, sx, gx, sh0, sh1, gh0, gh1,
+           pa, pb, rinv, sx, gx, sh0, sh1, gh0, gh1,
            in_sem, snd_sem, got_sem, hs_sem, hg_sem):
     edge = h.shape[1] - 2 * TOP
     sh, gh = (sh0, sh1), (gh0, gh1)
@@ -192,41 +252,6 @@
 
                 lax.fori_loop(0, edge, one, 0, unroll=8)
 
-    lanes = lax.broadcasted_iota(jnp.int32, (edge, LANES), 1)
-    xs = lax.broadcasted_iota(jnp.int32, (edge, LANES), 0)
-    even = (lanes + xs) % 2 == 0
-    low_edge, high_edge = lanes == 0, lanes == LANES - 1
-
-    def near(ref, y):
-        centre = ref[y + 1, TOP:TOP + edge, :]
-        return centre, [
-            ref[y + 1, TOP - 1:TOP - 1 + edge, :],
-            ref[y + 1, TOP + 1:TOP + 1 + edge, :],
-            ref[y, TOP:TOP + edge, :],
-            ref[y + 2, TOP:TOP + edge, :],
-            jnp.where(low_edge, 0.0, pltpu.roll(centre, 1, 1)),
-            jnp.where(high_edge, 0.0, pltpu.roll(centre, LANES - 1, 1)),
-        ]
-
-    def sums(ref, y, with_s):
-        p0, p_near = near(ref, y)
-        h0, h_near = near(h, y)
-        flow, weight = None, None
-        for p_n, h_n in zip(p_near, h_near):
-            beta = h0 + h_n
-            flow = beta * p_n if flow is None else flow + beta * p_n
-            if with_s:
-                weight = beta if weight is None else weight + beta
-        return p0, flow, weight
-
-    def pass_over(body):
-        def step(i, _):
-            for j in range(2):
-                body(i * 2 + j, even if j == 0 else jnp.logical_not(even))
-            return 0
-
-        lax.fori_loop(0, edge // 2, step, 0)
-
     def keep(ref, slot, y, value):
         ref[y + 1, TOP:TOP + edge, :] = value
         sh[slot][2, pl.ds(y, 1), :] = value[0:1]
@@ -236,21 +261,17 @@
     unpack(lambda w: gx.at[w], ((pa, 0), (h, edge)))
 
     def red(y, mask):
-        p0, flow, weight = sums(pa, y, True)
+        p0, flow, weight = sums(pa, h, y, True)
         inverse = 1.0 / weight
         s[y] = weight
         rinv[y] = inverse
         keep(pb, 0, y, jnp.where(mask, (f[y] + flow) * inverse, p0))
 
     def black(y, mask):
-        p0, flow, _ = sums(pb, y, False)
+        p0, flow, _ = sums(pb, h, y, False)
         value = jnp.where(mask, p0, (f[y] + flow) * rinv[y])
         keep(pc, 1, y, value)
         out_p[pl.ds(y, edge, stride=edge), :] = value
-
-    def rest(y, mask):
-        p0, flow, _ = sums(pc, y, False)
-        out_r[pl.ds(y, edge, stride=edge), :] = f[y] - (s[y] * p0 - flow)
 
     def exchange(ref, slot):
         for side in range(2):
@@ -261,11 +282,10 @@
         receive(*ends, slot + 1)
         unpack(lambda w: gh[slot].at[w], ((ref, 0),))
 
-    pass_over(red)
+    pass_over(edge, red)
     exchange(pb, 0)
-    pass_over(black)
+    pass_over(edge, black)
     exchange(pc, 1)
-    pass_over(rest)
 
     for i in range(3):
         @pl.when(has_next)
@@ -280,26 +300,37 @@
     slots, edge, width = old_fields.shape[1:]
     held = slots * 3 // 4
     vmem = lambda *shape: pltpu.VMEM(shape, jnp.float32)
-    padded = vmem(edge + 2, edge + 2 * TOP, LANES)
-    block = vmem(edge, edge, LANES)
-    out = jax.ShapeDtypeStruct((edge * edge, LANES), jnp.float32)
-    pressure, residual = pl.pallas_call(
+    array = lambda *shape: jax.ShapeDtypeStruct(shape, jnp.float32)
+    near_shape, block = (edge + 2, edge + 2 * TOP, LANES), (edge, edge, LANES)
+    out = array(edge * edge, LANES)
+    in_vmem = pl.BlockSpec(memory_space=pltpu.VMEM)
+    state = pl.pallas_call(
         functools.partial(kernel, n_grp, n_dev),
-        out_shape=(out, out),
-        in_specs=[pl.BlockSpec(memory_space=pltpu.SMEM), pl.BlockSpec(memory_space=pl.ANY)],
-        out_specs=[pl.BlockSpec(memory_space=pltpu.VMEM)] * 2,
+        out_shape=(out, array(*near_shape), array(*near_shape), array(*block), array(*block)),
+        in_specs=[pl.BlockSpec(memory_space=pltpu.SMEM), pl.BlockSpec(memory_space=pltpu.HBM)],
+        out_specs=[in_vmem] * 5,
         scratch_shapes=[vmem(held, edge, width)] * 3
         + [vmem(2, edge, width), vmem(edge, width), vmem(2, edge, width)] * 2
-        + [padded] * 4 + [block] * 3
+        + [vmem(*near_shape)] * 2 + [vmem(*block)]
         + [vmem(4, 2 * edge, LANES)] * 2 + [vmem(4, edge, LANES)] * 4
         + [pltpu.SemaphoreType.DMA((3,))] * 3 + [pltpu.SemaphoreType.DMA((3, 4))] * 2,
         compiler_params=pltpu.CompilerParams(
-            collective_id=0, has_side_effects=True, vmem_limit_bytes=40 * 1024 * 1024),
+            collective_id=0, has_side_effects=True, vmem_limit_bytes=49 * 1024 * 1024),
         cost_estimate=pl.CostEstimate(
             flops=edge * edge * LANES * 80, bytes_accessed=4 * 1024 * 1024, transcendentals=0),
     )(old_counts, old_fields)
-    shape = (edge, edge, LANES)
-    return pressure.reshape(shape), residual.reshape(shape)
+    in_hbm = pl.BlockSpec(memory_space=pltpu.HBM)
+    pressure, residual = pl.pallas_call(
+        finish_kernel,
+        out_shape=(out, out),
+        in_specs=[in_vmem] * 5,
+        out_specs=[in_hbm] * 2,
+        scratch_shapes=[vmem(edge * edge, LANES), pltpu.SemaphoreType.DMA((2,))],
+        compiler_params=pltpu.CompilerParams(vmem_limit_bytes=16 * 1024 * 1024),
+        cost_estimate=pl.CostEstimate(
+            flops=edge * edge * LANES * 20, bytes_accessed=4 * 1024 * 1024, transcendentals=0),
+    )(*state)
+    return pressure.reshape(block), residual.reshape(block)
 
 
 def solution(mesh):

time: 33.8 us -> 28 us (0.83)
  local copies, waits for them, and re-layouts: 4.13 us -> 0.65 us
  Pallas kernels: 28.9 us -> 26.6 us
    unnamed x6 -> x2, local copies, waits for them, and re-layouts: 4.13 us -> 0.65 us
    pallas_call x1 -> x2, Pallas kernels: 28.9 us -> 26.6 us  [the longest x1 24.7 us: per_device(): pl.pallas_call(functools.partial(kernel, n_grp, n_dev), out_shape=(out, a...]
where the time goes in v2:
time: 28 us; the launch traced here: 27.9 us
  Pallas kernels  26.6 us (95%)
  local copies, waits for them, and re-layouts  0.65 us (2%)
  between operations  0.65 us (2%)
    pallas_call x1, Pallas kernels, per_device(): pl.pallas_call(functools.partial(kernel, n_grp, n_dev), out_shape=(out, a...  24.7 us
    pallas_call x1, Pallas kernels, per_device(): pl.pallas_call(finish_kernel, out_shape=(out, out), in_specs=[in_vmem] *...  1.81 us
    unnamed x2, local copies, waits for them, and re-layouts  0.65 us

profile of v2, /device:TPU:0, one launch (start us, length us, event | category | flops | bytes accessed | tf_op | source)
XLA Modules:
  0.0 27.9 jit_solution(9725722144184969356)
XLA Ops:
  0.6 0.0 copy-start
  0.6 0.6 %copy-done = s32[32]{0:T(128)S(1)} copy-done((s32[32]{0:T(128)S(1)}, s32[32]{0:T(128)}, u32[]{:S(2)}) %copy-start) | copy-done | bytes 152
  1.3 24.7 %shard_map.41 = (f32[1024,128]{1,0:T(8,128)S(1)}, f32[34,48,128]{2,1,0:T(8,128)S(1)}, f32[34,48,128]{2,1,0:T(8,128)S(1)}, f32[32,32,128]{2,1,0:T(8,128)S(1)}, f32[32,32,128]{2,1,0:T(8,128)S(1)}) custom-call(s32[32]{0:T(128)S(1)} %copy-done, f32[3,8,32,1024]{3,2,1,0:T(8,128)} %fields.1), custom_call_target="tpu_custom_call" | custom-call | flops 10485760 | bytes 4194304 | tf_op jit(solution)/shard_map/pallas_call | solution.py:307
  26.0 1.8 %shard_map.42 = (f32[1024,128]{1,0:T(8,128)}, f32[1024,128]{1,0:T(8,128)}) custom-call(f32[1024,128]{1,0:T(8,128)S(1)} %get-tuple-element.9.pressure, f32[34,48,128]{2,1,0:T(8,128)S(1)} %get-tuple-element.10.pc, f32[34,48,128]{2,1,0:T(8,128)S(1)} %get-tuple-element.11.h, f32[32,32,128]{2,1,0:T(8,128)S(1)} %get-tuple-element.12.f, ...), custom_call_target="tpu_custom_call" | custom-call | flops 2621440 | bytes 4194304 | tf_op jit(solution)/shard_map/pallas_call | solution.py:323
Async XLA Ops:
  0.6 0.7 %copy-start = (s32[32]{0:T(128)S(1)}, s32[32]{0:T(128)}, u32[]{:S(2)}) copy-start(s32[32]{0:T(128)} %counts.1) | copy-start | bytes 388

commit v3 on v2

--- a/solution.py
+++ b/solution.py
@@ -33,9 +33,33 @@
     ]
 
 
-def sums(ref, h, y, with_s):
-    p0, p_near = near(ref, y)
-    h0, h_near = near(h, y)
+def rows_of(ref):
+    return ref.reshape(ref.shape[0] * ref.shape[1], LANES)
+
+
+def across(ref, x, y=0):
+    pitch, edge = ref.shape[1], ref.shape[0] - 2
+    return pl.ds((y + 1) * pitch + TOP + x, edge, stride=pitch)
+
+
+def near_x(ref, x):
+    edge = ref.shape[0] - 2
+    lanes = lax.broadcasted_iota(jnp.int32, (edge, LANES), 1)
+    rows = rows_of(ref)
+    centre = rows[across(ref, x), :]
+    return centre, [
+        rows[across(ref, x - 1), :],
+        rows[across(ref, x + 1), :],
+        rows[across(ref, x, -1), :],
+        rows[across(ref, x, 1), :],
+        jnp.where(lanes == 0, 0.0, pltpu.roll(centre, 1, 1)),
+        jnp.where(lanes == LANES - 1, 0.0, pltpu.roll(centre, LANES - 1, 1)),
+    ]
+
+
+def sums(ref, h, y, with_s, nearby=near):
+    p0, p_near = nearby(ref, y)
+    h0, h_near = nearby(h, y)
     flow, weight = None, None
     for p_n, h_n in zip(p_near, h_near):
         beta = h0 + h_n
@@ -111,14 +135,13 @@
     start = lax.fori_loop(0, me, lambda i, acc: acc + counts[i], jnp.int32(0))
     k = jnp.clip(start - me * 4, 0, 2)
 
-    zero_plane = jnp.zeros(h.shape[1:], jnp.float32)
-
-    def clear(y, _):
-        for ref in (pa, pb, pc, h):
-            ref[y] = zero_plane
-        return 0
-
-    lax.fori_loop(0, edge + 2, clear, 0)
+    no_face = jnp.zeros((edge, LANES), jnp.float32)
+    for ref in (pa, pb, pc, h):
+        ref[0, TOP:TOP + edge, :] = no_face
+        ref[edge + 1, TOP:TOP + edge, :] = no_face
+        rows_of(ref)[across(ref, -1), :] = no_face
+        rows_of(ref)[across(ref, edge), :] = no_face
+
     pl.semaphore_wait(barrier, total)
 
     lane = lax.broadcasted_iota(jnp.int32, (8, 1024), 1)
@@ -184,19 +207,19 @@
                 if i == 2:
                     f[y] = rows[j]
                 else:
-                    ref, value, at = (h, 0.5 * rows[j], edge) if i == 0 else (pa, rows[j], 0)
+                    ref, value = (h, 0.5 * rows[j]) if i == 0 else (pa, rows[j])
                     ref[y + 1, TOP:TOP + edge, :] = value
-                    for side in range(2):
-                        sx[side + 2, pl.ds(at + y, 1), :] = (
-                            value[0:1] if side == 0 else value[edge - 1:edge])
             return 0
 
-        lax.fori_loop(0, edge // 4, place, 0)
+        lax.fori_loop(0, edge // 4, place, 0, unroll=4)
         if i == 1:
             for side in range(2):
                 y = 1 if side == 0 else edge
                 sx[side, 0:edge, :] = pa[y, TOP:TOP + edge, :]
                 sx[side, edge:2 * edge, :] = h[y, TOP:TOP + edge, :]
+                x = 0 if side == 0 else edge - 1
+                sx[side + 2, 0:edge, :] = rows_of(pa)[across(pa, x), :]
+                sx[side + 2, edge:2 * edge, :] = rows_of(h)[across(h, x), :]
 
             def halo(src, dst, slot):
                 return [
@@ -241,51 +264,55 @@
                     ref[y, TOP:TOP + edge, :] = src(side)[at:at + edge, :]
 
         for side in range(2):
-            x = TOP - 1 if side == 0 else TOP + edge
+            x = -1 if side == 0 else edge
 
             @pl.when(has[side + 2])
             def _(side=side, x=x):
-                def one(y, _):
-                    for ref, at in targets:
-                        ref[y + 1, x:x + 1, :] = src(side + 2)[pl.ds(at + y, 1), :]
-                    return 0
-
-                lax.fori_loop(0, edge, one, 0, unroll=8)
-
-    def keep(ref, slot, y, value):
-        ref[y + 1, TOP:TOP + edge, :] = value
-        sh[slot][2, pl.ds(y, 1), :] = value[0:1]
-        sh[slot][3, pl.ds(y, 1), :] = value[edge - 1:edge]
+                for ref, at in targets:
+                    rows_of(ref)[across(ref, x), :] = src(side + 2)[at:at + edge, :]
 
     receive(*wide, 0)
     unpack(lambda w: gx.at[w], ((pa, 0), (h, edge)))
+
+    even = even_cells(edge)
 
     def red(y, mask):
         p0, flow, weight = sums(pa, h, y, True)
         inverse = 1.0 / weight
         s[y] = weight
         rinv[y] = inverse
-        keep(pb, 0, y, jnp.where(mask, (f[y] + flow) * inverse, p0))
+        pb[y + 1, TOP:TOP + edge, :] = jnp.where(mask, (f[y] + flow) * inverse, p0)
 
     def black(y, mask):
         p0, flow, _ = sums(pb, h, y, False)
         value = jnp.where(mask, p0, (f[y] + flow) * rinv[y])
-        keep(pc, 1, y, value)
+        pc[y + 1, TOP:TOP + edge, :] = value
         out_p[pl.ds(y, edge, stride=edge), :] = value
 
-    def exchange(ref, slot):
+    def send_faces(ref, slot):
         for side in range(2):
-            y = 1 if side == 0 else edge
-            sh[slot][side] = ref[y, TOP:TOP + edge, :]
-        ends = (lambda w: sh[slot].at[w], lambda w: gh[slot].at[w])
-        send(*ends, slot + 1)
-        receive(*ends, slot + 1)
+            at = 0 if side == 0 else edge - 1
+            is_red = even if at % 2 == 0 else jnp.logical_not(even)
+            thin = pl.ds(at, edge, stride=edge)
+            for w, nearby, rhs, inv in (
+                    (side, near, lambda: f[at], lambda: rinv[at]),
+                    (side + 2, near_x, lambda: rows_of(f)[thin, :], lambda: rows_of(rinv)[thin, :])):
+                p0, flow, weight = sums(ref, h, at, slot == 0, nearby)
+                inverse = 1.0 / weight if slot == 0 else inv()
+                value = (rhs() + flow) * inverse
+                sh[slot][w] = jnp.where(is_red, value, p0) if slot == 0 else jnp.where(is_red, p0, value)
+        send(lambda w: sh[slot].at[w], lambda w: gh[slot].at[w], slot + 1)
+
+    def take_faces(ref, slot):
+        receive(lambda w: sh[slot].at[w], lambda w: gh[slot].at[w], slot + 1)
         unpack(lambda w: gh[slot].at[w], ((ref, 0),))
 
+    send_faces(pa, 0)
     pass_over(edge, red)
-    exchange(pb, 0)
+    take_faces(pb, 0)
+    send_faces(pb, 1)
     pass_over(edge, black)
-    exchange(pc, 1)
+    take_faces(pc, 1)
 
     for i in range(3):
         @pl.when(has_next)

time: 28 us -> 25.6 us (0.914)
  Pallas kernels: 26.6 us -> 24.2 us
    pallas_call x1, Pallas kernels: 24.7 us -> 22.3 us  [per_device(): pl.pallas_call(functools.partial(kernel, n_grp, n_dev), out_shape=(out, a...]
where the time goes in v3:
time: 25.6 us; the launch traced here: 25.4 us
  Pallas kernels  24.2 us (95%)
  local copies, waits for them, and re-layouts  0.65 us (3%)
  between operations  0.65 us (3%)
    pallas_call x1, Pallas kernels, per_device(): pl.pallas_call(functools.partial(kernel, n_grp, n_dev), out_shape=(out, a...  22.3 us
    pallas_call x1, Pallas kernels, per_device(): pl.pallas_call(finish_kernel, out_shape=(out, out), in_specs=[in_vmem] *...  1.81 us
    unnamed x2, local copies, waits for them, and re-layouts  0.65 us

profile of v3, /device:TPU:0, one launch (start us, length us, event | category | flops | bytes accessed | tf_op | source)
XLA Modules:
  0.0 25.4 jit_solution(2661179617359607291)
XLA Ops:
  0.6 0.0 copy-start
  0.6 0.6 %copy-done = s32[32]{0:T(128)S(1)} copy-done((s32[32]{0:T(128)S(1)}, s32[32]{0:T(128)}, u32[]{:S(2)}) %copy-start) | copy-done | bytes 152
  1.3 22.3 %shard_map.41 = (f32[1024,128]{1,0:T(8,128)S(1)}, f32[34,48,128]{2,1,0:T(8,128)S(1)}, f32[34,48,128]{2,1,0:T(8,128)S(1)}, f32[32,32,128]{2,1,0:T(8,128)S(1)}, f32[32,32,128]{2,1,0:T(8,128)S(1)}) custom-call(s32[32]{0:T(128)S(1)} %copy-done, f32[3,8,32,1024]{3,2,1,0:T(8,128)} %fields.1), custom_call_target="tpu_custom_call" | custom-call | flops 10485760 | bytes 4194304 | tf_op jit(solution)/shard_map/pallas_call | solution.py:334
  23.6 1.8 %shard_map.42 = (f32[1024,128]{1,0:T(8,128)}, f32[1024,128]{1,0:T(8,128)}) custom-call(f32[1024,128]{1,0:T(8,128)S(1)} %get-tuple-element.9.pressure, f32[34,48,128]{2,1,0:T(8,128)S(1)} %get-tuple-element.10.pc, f32[34,48,128]{2,1,0:T(8,128)S(1)} %get-tuple-element.11.h, f32[32,32,128]{2,1,0:T(8,128)S(1)} %get-tuple-element.12.f, ...), custom_call_target="tpu_custom_call" | custom-call | flops 2621440 | bytes 4194304 | tf_op jit(solution)/shard_map/pallas_call | solution.py:350
Async XLA Ops:
  0.6 0.7 %copy-start = (s32[32]{0:T(128)S(1)}, s32[32]{0:T(128)}, u32[]{:S(2)}) copy-start(s32[32]{0:T(128)} %counts.1) | copy-start | bytes 388

commit v4 on v3

--- a/solution.py
+++ b/solution.py
@@ -132,7 +132,8 @@
         def _(target=target):
             pl.semaphore_signal(barrier, inc=1, device_id=target, device_id_type=MESH)
 
-    start = lax.fori_loop(0, me, lambda i, acc: acc + counts[i], jnp.int32(0))
+    number = lax.broadcasted_iota(jnp.int32, counts.shape, 1)
+    start = jnp.sum(jnp.where(number < me, counts[...], 0))
     k = jnp.clip(start - me * 4, 0, 2)
 
     no_face = jnp.zeros((edge, LANES), jnp.float32)
@@ -334,7 +335,7 @@
     state = pl.pallas_call(
         functools.partial(kernel, n_grp, n_dev),
         out_shape=(out, array(*near_shape), array(*near_shape), array(*block), array(*block)),
-        in_specs=[pl.BlockSpec(memory_space=pltpu.SMEM), pl.BlockSpec(memory_space=pltpu.HBM)],
+        in_specs=[in_vmem, pl.BlockSpec(memory_space=pltpu.HBM)],
         out_specs=[in_vmem] * 5,
         scratch_shapes=[vmem(held, edge, width)] * 3
         + [vmem(2, edge, width), vmem(edge, width), vmem(2, edge, width)] * 2
@@ -345,7 +346,7 @@
             collective_id=0, has_side_effects=True, vmem_limit_bytes=49 * 1024 * 1024),
         cost_estimate=pl.CostEstimate(
             flops=edge * edge * LANES * 80, bytes_accessed=4 * 1024 * 1024, transcendentals=0),
-    )(old_counts, old_fields)
+    )(old_counts.reshape(1, -1), old_fields)
     in_hbm = pl.BlockSpec(memory_space=pltpu.HBM)
     pressure, residual = pl.pallas_call(
         finish_kernel,

time: 25.6 us -> 25 us (0.977)
  Pallas kernels: 24.2 us -> 23.6 us
    pallas_call x1, Pallas kernels: 22.3 us -> 21.8 us  [per_device(): pl.pallas_call(functools.partial(kernel, n_grp, n_dev), out_shape=(out, a...]
where the time goes in v4:
time: 25 us; the launch traced here: 24.9 us
  Pallas kernels  23.6 us (94%)
  local copies, waits for them, and re-layouts  0.65 us (3%)
  between operations  0.65 us (3%)
    pallas_call x1, Pallas kernels, per_device(): pl.pallas_call(functools.partial(kernel, n_grp, n_dev), out_shape=(out, a...  21.8 us
    pallas_call x1, Pallas kernels, per_device(): pl.pallas_call(finish_kernel, out_shape=(out, out), in_specs=[in_vmem] *...  1.81 us
    unnamed x2, local copies, waits for them, and re-layouts  0.65 us

profile of v4, /device:TPU:0, one launch (start us, length us, event | category | flops | bytes accessed | tf_op | source)
XLA Modules:
  0.0 24.9 jit_solution(10496921808261742934)
XLA Ops:
  0.6 0.0 copy-start
  0.6 0.6 %copy-done = s32[32]{0:T(128)S(1)} copy-done((s32[32]{0:T(128)S(1)}, s32[32]{0:T(128)}, u32[]{:S(2)}) %copy-start) | copy-done | bytes 152
  1.3 21.8 %shard_map.41 = (f32[1024,128]{1,0:T(8,128)S(1)}, f32[34,48,128]{2,1,0:T(8,128)S(1)}, f32[34,48,128]{2,1,0:T(8,128)S(1)}, f32[32,32,128]{2,1,0:T(8,128)S(1)}, f32[32,32,128]{2,1,0:T(8,128)S(1)}) custom-call(s32[1,32]{1,0:T(1,128)S(1)} %bitcast.3, f32[3,8,32,1024]{3,2,1,0:T(8,128)} %fields.1), custom_call_target="tpu_custom_call" | custom-call | flops 10485760 | bytes 4194304 | tf_op jit(solution)/shard_map/pallas_call | solution.py:335
  23.0 1.8 %shard_map.42 = (f32[1024,128]{1,0:T(8,128)}, f32[1024,128]{1,0:T(8,128)}) custom-call(f32[1024,128]{1,0:T(8,128)S(1)} %get-tuple-element.9.pressure, f32[34,48,128]{2,1,0:T(8,128)S(1)} %get-tuple-element.10.pc, f32[34,48,128]{2,1,0:T(8,128)S(1)} %get-tuple-element.11.h, f32[32,32,128]{2,1,0:T(8,128)S(1)} %get-tuple-element.12.f, ...), custom_call_target="tpu_custom_call" | custom-call | flops 2621440 | bytes 4194304 | tf_op jit(solution)/shard_map/pallas_call | solution.py:351
Async XLA Ops:
  0.6 0.7 %copy-start = (s32[32]{0:T(128)S(1)}, s32[32]{0:T(128)}, u32[]{:S(2)}) copy-start(s32[32]{0:T(128)} %param.3) | copy-start | bytes 388
